TPU v7x, 256 devices: a whole 4x4x8 slice. The times are simulated.
256 devices in a mesh: ctx: 32 (over z, x), head: 8 (over y, core).
Axes of the slice: x: 4, y: 4, z: 8, core: 2. Of those that a mesh axis runs over, the one named last changes fastest.
Arguments:
- query_rows: bfloat16 [32768, 6144], P(('ctx', 'head')), may hold values from -0.52734375 to 0.52734375
- key_rows: bfloat16 [32768, 6144], P(('ctx', 'head')), may hold values from -0.52734375 to 0.52734375
- value_rows: bfloat16 [32768, 6144], P(('ctx', 'head')), may hold values from -0.4453125 to 0.4453125
- grad_out: bfloat16 [32768, 6144], P(('ctx', 'head')), may hold values from -0.4453125 to 0.4453125
- decay_rates: float32 [48], replicated, as said below
Outputs:
- query_gradient: bfloat16 [32768, 6144], P(('ctx', 'head'))
- grad_key: bfloat16 [32768, 6144], P(('ctx', 'head'))
- value_gradient: bfloat16 [32768, 6144], P(('ctx', 'head'))
Inputs may be any that keep to these rules, and one draw needn't show every extreme that they name: decay_rates lie between 0.1 / 32768 and 24 / 256.
All inputs are finite; a program needn't handle non-finite values.
Results may differ from a plain program's by a relative error of at most 0.0056.
Values may be sent and summed in bfloat16 or wider, within the bound.
A program may use at most 128 MiB of HBM per device.

v0:
```python
import jax
import jax.numpy as jnp
from jax import lax
from jax.experimental import pallas as pl
from jax.experimental.pallas import tpu as pltpu
from jax.sharding import PartitionSpec as P

DH = 128
ROWS = 128
LINES = 32
YS = 4
HEADS = 48
H = 2
CHUNKS = HEADS // (8 * H)
STATES = 2 * H
PART = STATES * DH // LINES
MESH = pl.DeviceIdType.MESH
F32 = jnp.float32
BF16 = jnp.bfloat16


def dot(a, b, dims):
    return lax.dot_general(a, b, ((dims[:1], dims[1:]), ((), ())), preferred_element_type=F32)


def row_index():
    return lax.broadcasted_iota(jnp.int32, (ROWS, DH), 0).astype(F32)


def kernel(
    rates, q_hbm, k_hbm, v_hbm, g_hbm, dq_hbm, dk_hbm, dv_hbm,
    q, k, v, g, dq, dk, dv, dq_in, dk_in, dv_in,
    own_local, c_send, c_recv, y_send, y_recv, t_send, t_recv, b_send, b_recv,
    s_send, s_recv, s_own, x_send, x_recv,
    load_sem, store_sem, cs, cr, ys, yr, ts, tr, bs, br, ss, sr, xs, xr,
):
    line, place = lax.axis_index("ctx"), lax.axis_index("head")
    y, core = place // 2, place % 2
    sibling = (line, place + 1 - 2 * core)

    def along_y(other):
        return (line, other * 2 + core)

    def across(other):
        return (other, place)

    ins = ((k_hbm, k), (v_hbm, v), (q_hbm, q), (g_hbm, g))
    outs = ((dq, dq_hbm), (dk, dk_hbm), (dv, dv_hbm))
    width = 8 * H * DH

    def load(c, n):
        cols = pl.ds(c * width, width)
        return pltpu.make_async_copy(ins[n][0].at[:, cols], ins[n][1].at[:, cols], load_sem.at[c, n])

    def store(c, n):
        cols = pl.ds(c * width, width)
        return pltpu.make_async_copy(outs[n][0].at[:, cols], outs[n][1].at[:, cols], store_sem.at[c, n])

    for c in range(CHUNKS):
        for n in range(4):
            load(c, n).start()

    barrier = pltpu.get_barrier_semaphore()
    pl.semaphore_signal(barrier, inc=1, device_id=sibling, device_id_type=MESH)
    for d in range(1, YS):
        pl.semaphore_signal(barrier, inc=1, device_id=along_y((y + d) % YS), device_id_type=MESH)

    def greet(d, carry):
        pl.semaphore_signal(barrier, inc=1, device_id=across((line + d) % LINES), device_id_type=MESH)
        return carry

    lax.fori_loop(1, LINES, greet, 0)

    def head_of(c, which, owner, e):
        return c * 8 * H + which * 4 * H + owner * H + e

    def cols_of(head):
        return pl.ds(pl.multiple_of(head * DH, DH), DH)

    def remote(src, dst, send, recv, device):
        return pltpu.make_async_remote_copy(
            src_ref=src, dst_ref=dst, send_sem=send, recv_sem=recv, device_id=device, device_id_type=MESH
        )

    def wait_bytes(ref, sem):
        pltpu.make_async_copy(ref, ref, sem).wait()

    def local_states(head):
        r = rates[head]
        cols = cols_of(head)
        row = row_index()
        kd = (k[:, cols].astype(F32) * jnp.exp(-r * (ROWS - 1.0 - row))).astype(BF16)
        qd = (q[:, cols].astype(F32) * jnp.exp(-r * row)).astype(BF16)
        return dot(kd, v[:, cols], (0, 0)), dot(qd, g[:, cols], (0, 0))

    def locals_of(c):
        for n in range(4):
            load(c, n).wait()

        def theirs(i, carry):
            owner, e = i // H, i % H
            kv, qd = local_states(head_of(c, 1 - core, owner, e))
            c_send[c, owner, e] = kv.astype(BF16)
            c_send[c, owner, H + e] = qd.astype(BF16)
            return carry

        lax.fori_loop(0, 4 * H, theirs, 0, unroll=4)
        if c == 0:
            pl.semaphore_wait(barrier, 1 + (YS - 1) + (LINES - 1))
        remote(c_send.at[c], c_recv.at[c], cs.at[c], cr.at[c], sibling).start()

        def mine(i, carry):
            owner, e = i // H, i % H
            kv, qd = local_states(head_of(c, core, owner, e))
            own_local[c, owner, e] = kv
            own_local[c, owner, H + e] = qd
            return carry

        lax.fori_loop(0, 4 * H, mine, 0, unroll=4)

    def decay(r, steps):
        return jnp.exp(jnp.full((1, DH), -r * steps, F32))

    def send_y(c):
        wait_bytes(c_recv.at[c], cr.at[c])
        for d in (2, 1, 3, 0):
            owner = (y + d) % YS
            target = y_recv.at[c, y] if d == 0 else y_send.at[c, owner]
            for e in range(H):
                half = decay(rates[head_of(c, core, owner, e)], float(ROWS))
                one = jnp.ones_like(half)
                for way in range(2):
                    s = way * H + e
                    early = core == way
                    a = jnp.where(early, half, one)
                    b = jnp.where(early, one, half)
                    target[s] = (a * own_local[c, owner, s] + b * c_recv[c, owner, s].astype(F32)).astype(BF16)
            if d != 0:
                remote(y_send.at[c, owner], y_recv.at[c, y], ys.at[c], yr.at[c], along_y(owner)).start()

    def horner(c, s, rows, start):
        way, e = s // H, s % H
        a = decay(rates[head_of(c, core, y, e)], 2.0 * ROWS)
        order = range(YS) if way == 0 else range(YS - 1, -1, -1)
        state, states = start, []
        for chip in order:
            states.append((chip, state))
            term = y_recv[c, chip, s, rows].astype(F32)
            state = term if state is None else a * state + term
        return states, state

    def send_lines(c):
        wait_bytes(y_recv.at[c, pl.ds(0, YS - 1)], yr.at[c])
        for s in range(STATES):
            for part in range(2):
                rows = pl.ds(part * 64, 64)
                t_send[c, s, rows] = horner(c, s, rows, None)[1].astype(BF16)
        per = DH // PART

        def rows_of(ref, p):
            return ref.at[c, p // per, pl.ds(pl.multiple_of((p % per) * PART, PART), PART)]

        def go(d, carry):
            p = (line + d) % LINES
            remote(rows_of(t_send, p), t_recv.at[c, line], ts.at[c], tr.at[c], across(p)).start()
            return carry

        lax.fori_loop(1, LINES, go, 0)
        t_recv[c, line] = rows_of(t_send, line)[...]

    def scan_lines(c):
        wait_bytes(t_recv.at[c, pl.ds(0, LINES - 1)], tr.at[c])
        per = DH // PART
        way, e = line // (LINES // 2), (line // per) % H
        a = decay(rates[head_of(c, core, y, e)], 2.0 * ROWS * YS)

        def step(i, state):
            at = jnp.where(way == 0, i, LINES - 1 - i)
            b_send[c, at] = state.astype(BF16)
            return a * state + t_recv[c, at].astype(F32)

        lax.fori_loop(0, LINES, step, jnp.zeros((PART, DH), F32), unroll=8)

        def rows_of(ref, p):
            return ref.at[c, p // per, pl.ds(pl.multiple_of((p % per) * PART, PART), PART)]

        def go(d, carry):
            p = (line + d) % LINES
            remote(b_send.at[c, p], rows_of(b_recv, line), bs.at[c], br.at[c], across(p)).start()
            return carry

        lax.fori_loop(1, LINES, go, 0)
        rows_of(b_recv, line)[...] = b_send[c, line]

    def send_states(c):
        wait_bytes(t_recv.at[c, pl.ds(0, LINES - 1)], br.at[c])
        for s in range(STATES):
            for part in range(2):
                rows = pl.ds(part * 64, 64)
                for chip, state in horner(c, s, rows, b_recv[c, s, rows].astype(F32))[0]:
                    s_send[c, chip, s, rows] = state.astype(BF16)
        for d in (2, 1, 3):
            chip = (y + d) % YS
            remote(s_send.at[c, chip], s_recv.at[c, y], ss.at[c], sr.at[c], along_y(chip)).start()

    def send_sibling(c):
        wait_bytes(s_recv.at[c, pl.ds(0, YS - 1)], sr.at[c])
        near = 1 - core
        for d in range(YS):
            owner = (y + d) % YS
            source = s_send.at[c, y] if d == 0 else s_recv.at[c, owner]
            for e in range(H):
                half = decay(rates[head_of(c, core, owner, e)], float(ROWS))
                s = near * H + e
                state = source[s]
                s_own[c, owner, s] = (half * state.astype(F32) + c_recv[c, owner, s].astype(F32)).astype(BF16)
                x_send[c, owner, s] = state
                s = core * H + e
                state = source[s]
                s_own[c, owner, s] = state
                x_send[c, owner, s] = (half * state.astype(F32) + own_local[c, owner, s]).astype(BF16)
        remote(x_send.at[c], x_recv.at[c], xs.at[c], xr.at[c], sibling).start()

    def inside(first, count):
        def one(head, carry):
            r = rates[head]
            cols = cols_of(head)
            gap = row_index() - lax.broadcasted_iota(jnp.int32, (ROWS, DH), 1).astype(F32)
            mask = jnp.where(gap >= 0.0, jnp.exp(-r * jnp.maximum(gap, 0.0)), 0.0)
            kh, vh, qh, gh = k[:, cols], v[:, cols], q[:, cols], g[:, cols]
            weights = (dot(gh, vh, (1, 1)) * mask).astype(BF16)
            forward = (dot(qh, kh, (1, 1)) * mask).astype(BF16)
            dq_in[:, cols] = dot(weights, kh, (1, 0))
            dk_in[:, cols] = dot(weights, qh, (0, 0))
            dv_in[:, cols] = dot(forward, gh, (0, 0))
            return carry

        lax.fori_loop(first, first + count, one, 0, unroll=2)

    def finish(c, which, states):
        def one(i, carry):
            owner, e = i // H, i % H
            head = head_of(c, which, owner, e)
            r = rates[head]
            cols = cols_of(head)
            row = row_index()
            lead = jnp.exp(-r * (row + 1.0))
            trail = jnp.exp(-r * (ROWS - row))
            before, after = states[c, owner, e], states[c, owner, H + e]
            dq[:, cols] = (dq_in[:, cols] + lead * dot(g[:, cols], before, (1, 1))).astype(BF16)
            dk[:, cols] = (dk_in[:, cols] + trail * dot(v[:, cols], after, (1, 1))).astype(BF16)
            dv[:, cols] = (dv_in[:, cols] + trail * dot(k[:, cols], after, (1, 0))).astype(BF16)
            return carry

        lax.fori_loop(0, 4 * H, one, 0, unroll=2)

    def finish_all(c):
        finish(c, core, s_own)
        wait_bytes(x_recv.at[c], xr.at[c])
        finish(c, 1 - core, x_recv)
        for n in range(3):
            store(c, n).start()

    locals_of(0)
    locals_of(1)
    send_y(0)
    locals_of(2)
    send_y(1)
    inside(0, 8)
    send_y(2)
    inside(8, 8)
    send_lines(0)
    inside(16, 8)
    send_lines(1)
    scan_lines(0)
    inside(24, 8)
    send_lines(2)
    scan_lines(1)
    inside(32, 8)
    send_states(0)
    scan_lines(2)
    inside(40, 8)
    send_states(1)
    send_states(2)
    send_sibling(0)
    finish_all(0)
    send_sibling(1)
    finish_all(1)
    send_sibling(2)
    finish_all(2)

    for c in range(CHUNKS):
        for n in range(3):
            store(c, n).wait()
        wait_bytes(c_send.at[c], cs.at[c])
        wait_bytes(y_send.at[c, pl.ds(0, YS - 1)], ys.at[c])
        wait_bytes(t_recv.at[c, pl.ds(0, LINES - 1)], ts.at[c])
        wait_bytes(b_send.at[c, pl.ds(0, LINES - 1)], bs.at[c])
        wait_bytes(s_send.at[c, pl.ds(0, YS - 1)], ss.at[c])
        wait_bytes(x_send.at[c], xs.at[c])


def local(query_rows, key_rows, value_rows, grad_out, decay_rates):
    whole = (ROWS, HEADS * DH)
    quad = (CHUNKS, YS, STATES, DH, DH)
    sems = pltpu.SemaphoreType.DMA((CHUNKS,))
    anywhere = pl.BlockSpec(memory_space=pl.ANY)
    return pl.pallas_call(
        kernel,
        out_shape=[jax.ShapeDtypeStruct(whole, BF16)] * 3,
        in_specs=[pl.BlockSpec(memory_space=pltpu.SMEM)] + [anywhere] * 4,
        out_specs=[anywhere] * 3,
        scratch_shapes=[pltpu.VMEM(whole, BF16)] * 7
        + [pltpu.VMEM(whole, F32)] * 3
        + [
            pltpu.VMEM(quad, F32),
            pltpu.VMEM(quad, BF16),
            pltpu.VMEM(quad, BF16),
            pltpu.VMEM(quad, BF16),
            pltpu.VMEM(quad, BF16),
            pltpu.VMEM((CHUNKS, STATES, DH, DH), BF16),
            pltpu.VMEM((CHUNKS, LINES, PART, DH), BF16),
            pltpu.VMEM((CHUNKS, LINES, PART, DH), BF16),
            pltpu.VMEM((CHUNKS, STATES, DH, DH), BF16),
            pltpu.VMEM(quad, BF16),
            pltpu.VMEM(quad, BF16),
            pltpu.VMEM(quad, BF16),
            pltpu.VMEM(quad, BF16),
            pltpu.VMEM(quad, BF16),
            pltpu.SemaphoreType.DMA((CHUNKS, 4)),
            pltpu.SemaphoreType.DMA((CHUNKS, 3)),
        ]
        + [sems] * 12,
        compiler_params=pltpu.CompilerParams(
            collective_id=0, has_side_effects=True, vmem_limit_bytes=60 * 1024 * 1024
        ),
        name="decayed_attention_backward",
    )(decay_rates, query_rows, key_rows, value_rows, grad_out)


def solution(mesh):
    rows = P(("ctx", "head"), None)
    return jax.shard_map(
        local,
        mesh=mesh,
        in_specs=(rows, rows, rows, rows, P()),
        out_specs=(rows, rows, rows),
        check_vma=False,
    )
```

profile of v0, /device:TPU:1, one launch (start us, length us, event | category | flops | bytes accessed | tf_op | source)
XLA Modules:
  0.0 67.7 jit_solution(11541355966696316500)
XLA Ops:
  0.6 61.1 %decayed_attention_backward.1 = (bf16[128,6144]{1,0:T(8,128)(2,1)}, bf16[128,6144]{1,0:T(8,128)(2,1)}, bf16[128,6144]{1,0:T(8,128)(2,1)}) custom-call(f32[48]{0:T(128)} %rates.1, bf16[128,6144]{1,0:T(8,128)(2,1)} %q_hbm.1, bf16[128,6144]{1,0:T(8,128)(2,1)} %k_hbm.1, bf16[128,6144]{1,0:T(8,128)(2,1)} %v_hbm.1, bf16[128,6144]{1,0:T(8,128)(2,1)} %g_hbm.1), custom_call_target="tpu_custom_call" | custom-call | tf_op jit(solution)/shard_map/decayed_attention_backward/pallas_call | solution.py:308
  61.7 0.0 copy-start.1
  61.7 2.8 %copy.11 = bf16[128,6144]{1,0:T(8,128)(2,1)} copy(bf16[128,6144]{1,0:T(8,128)(2,1)} %get-tuple-element.6) | data formatting | bytes 3145728
  64.5 0.0 copy-done.1
  64.5 0.0 copy-start
  64.5 1.1 %copy.12 = bf16[128,6144]{1,0:T(8,128)(2,1)} copy(bf16[128,6144]{1,0:T(8,128)(2,1)S(1)} %copy-done.1) | data formatting | bytes 3145728
  65.7 0.8 %copy-done = bf16[128,6144]{1,0:T(8,128)(2,1)S(1)} copy-done((bf16[128,6144]{1,0:T(8,128)(2,1)S(1)}, bf16[128,6144]{1,0:T(8,128)(2,1)}, u32[]{:S(2)}) %copy-start) | copy-done | bytes 1572888
  66.5 1.1 %copy.13 = bf16[128,6144]{1,0:T(8,128)(2,1)} copy(bf16[128,6144]{1,0:T(8,128)(2,1)S(1)} %copy-done) | data formatting | bytes 3145728
Async XLA Ops:
  61.7 2.8 %copy-start.1 = (bf16[128,6144]{1,0:T(8,128)(2,1)S(1)}, bf16[128,6144]{1,0:T(8,128)(2,1)}, u32[]{:S(2)}) copy-start(bf16[128,6144]{1,0:T(8,128)(2,1)} %get-tuple-element.7) | copy-start | bytes 4718596
  64.5 2.0 %copy-start = (bf16[128,6144]{1,0:T(8,128)(2,1)S(1)}, bf16[128,6144]{1,0:T(8,128)(2,1)}, u32[]{:S(2)}) copy-start(bf16[128,6144]{1,0:T(8,128)(2,1)} %get-tuple-element.8) | copy-start | bytes 4718596
where the time goes:
time: 67.8 us; the launch traced here: 67.7 us
  Pallas kernels  61.1 us (90%)
  local copies, waits for them, and re-layouts  5.93 us (9%)
    pallas_call x1, Pallas kernels, local(): pl.pallas_call(kernel, out_shape=[jax.ShapeDtypeStruct(whole, BF16)] * 3,...  61.1 us
    unnamed x7, local copies, waits for them, and re-layouts  5.93 us

commit v1 on v0

v1 whole, which is shorter than its diff:
```python
import jax
import jax.numpy as jnp
from jax import lax
from jax.experimental import pallas as pl
from jax.experimental.pallas import tpu as pltpu
from jax.sharding import PartitionSpec as P

DH = 128
ROWS = 128
HEADS = 48
XS, YS, ZS = 4, 4, 8
CHIPS = XS * YS
CHUNKS = HEADS // (2 * YS)
SLICE = 2 * DH // XS
MESH = pl.DeviceIdType.MESH
F32 = jnp.float32
BF16 = jnp.bfloat16


def dot(a, b, dims):
    return lax.dot_general(a, b, ((dims[:1], dims[1:]), ((), ())), preferred_element_type=F32)


def row_index():
    return lax.broadcasted_iota(jnp.int32, (ROWS, DH), 0).astype(F32)


def decay(r, steps):
    return jnp.exp(jnp.full((1, DH), -r * steps, F32))


def remote(src, dst, send, recv, device):
    return pltpu.make_async_remote_copy(
        src_ref=src, dst_ref=dst, send_sem=send, recv_sem=recv, device_id=device, device_id_type=MESH
    )


def wait_bytes(ref, sem):
    pltpu.make_async_copy(ref, ref, sem).wait()


def kernel(
    rates, q_hbm, k_hbm, v_hbm, g_hbm, dq, dk, dv,
    q, k, v, g, dq_in, dk_in, dv_in,
    own_local, c_send, c_recv, e_send, e_recv, l_send, l_recv, z_send, z_recv, s_send, s_recv, x_recv,
    load_sem, cs, cr, es, er, ls, lr, zs, zr, ss, sr, xs, xr,
):
    line, place = lax.axis_index("ctx"), lax.axis_index("head")
    z, x = line // XS, line % XS
    y, core = place // 2, place % 2
    chip = x * YS + y
    sibling = (line, place + 1 - 2 * core)
    way = x // 2
    turn = jnp.where(way == 0, z, ZS - 1 - z)

    def in_plane(to_x, to_y):
        return (z * XS + to_x, to_y * 2 + core)

    def along_z(to_z):
        return (to_z * XS + x, place)

    ins = ((k_hbm, k), (v_hbm, v), (q_hbm, q), (g_hbm, g))

    def load(c, n):
        cols = pl.ds(c * 2 * YS * DH, 2 * YS * DH)
        return pltpu.make_async_copy(ins[n][0].at[:, cols], ins[n][1].at[:, cols], load_sem.at[c, n])

    for c in range(CHUNKS):
        for n in range(4):
            load(c, n).start()

    barrier = pltpu.get_barrier_semaphore()
    pl.semaphore_signal(barrier, inc=1, device_id=sibling, device_id_type=MESH)

    def greet_plane(d, carry):
        to = in_plane((x + d // YS) % XS, (y + d % YS) % YS)
        pl.semaphore_signal(barrier, inc=1, device_id=to, device_id_type=MESH)
        return carry

    def greet_z(d, carry):
        pl.semaphore_signal(barrier, inc=1, device_id=along_z((z + d) % ZS), device_id_type=MESH)
        return carry

    lax.fori_loop(1, CHIPS, greet_plane, 0)
    lax.fori_loop(1, ZS, greet_z, 0)

    def head_of(c, which, owner):
        return (c * 2 + which) * YS + owner

    def cols_of(head):
        return pl.ds(pl.multiple_of(head * DH, DH), DH)

    def slice_of(index):
        return pl.ds(pl.multiple_of(index * SLICE, SLICE), SLICE)

    def local_states(head):
        r = rates[head]
        cols = cols_of(head)
        row = row_index()
        kd = (k[:, cols].astype(F32) * jnp.exp(-r * (ROWS - 1.0 - row))).astype(BF16)
        qd = (q[:, cols].astype(F32) * jnp.exp(-r * row)).astype(BF16)
        return dot(kd, v[:, cols], (0, 0)), dot(qd, g[:, cols], (0, 0))

    def locals_of(c):
        for n in range(4):
            load(c, n).wait()

        def theirs(owner, carry):
            kv, qd = local_states(head_of(c, 1 - core, owner))
            c_send[c, 0, owner] = kv.astype(BF16)
            c_send[c, 1, owner] = qd.astype(BF16)
            return carry

        lax.fori_loop(0, YS, theirs, 0, unroll=True)
        if c == 0:
            pl.semaphore_wait(barrier, 1 + (CHIPS - 1) + (ZS - 1))
        remote(c_send.at[c], c_recv.at[c], cs.at[c], cr.at[c], sibling).start()

        def mine(owner, carry):
            kv, qd = local_states(head_of(c, core, owner))
            own_local[c, owner, 0] = kv
            own_local[c, owner, 1] = qd
            e_send[c, owner] = jnp.where(core == 0, kv, qd).astype(BF16)
            return carry

        lax.fori_loop(0, YS, mine, 0, unroll=True)
        remote(e_send.at[c], e_recv.at[c], es.at[c], er.at[c], sibling).start()

    def send_locals(c):
        wait_bytes(c_recv.at[c], cr.at[c])
        for dy in (2, 1, 3, 0):
            to_y = (y + dy) % YS
            half = decay(rates[head_of(c, core, to_y)], float(ROWS))
            one = jnp.ones_like(half)
            for w in range(2):
                a = jnp.where(core == w, half, one)
                b = jnp.where(core == w, one, half)
                both = a * own_local[c, to_y, w] + b * c_recv[c, w, to_y].astype(F32)
                l_send[c, to_y, pl.ds(w * DH, DH)] = both.astype(BF16)
            for dx in (2, 1, 3, 0):
                to_x = (x + dx) % XS
                if dx or dy:
                    remote(
                        l_send.at[c, to_y, slice_of(to_x)], l_recv.at[c, chip], ls.at[c], lr.at[c],
                        in_plane(to_x, to_y),
                    ).start()
                else:
                    l_recv[c, chip] = l_send[c, y, slice_of(x)]

    def send_plane(c):
        wait_bytes(l_recv.at[c, pl.ds(0, CHIPS - 1)], lr.at[c])
        a = decay(rates[head_of(c, core, y)], 2.0 * ROWS)

        def step(i, state):
            return a * state + l_recv[c, jnp.where(way == 0, i, CHIPS - 1 - i)].astype(F32)

        z_send[c] = lax.fori_loop(0, CHIPS, step, jnp.zeros((SLICE, DH), F32), unroll=True)

        def go(i, carry):
            to_z = jnp.where(way == 0, i, ZS - 1 - i)
            remote(z_send.at[c], z_recv.at[c, z], zs.at[c, i], zr.at[c, z], along_z(to_z)).start()
            return carry

        lax.fori_loop(turn + 1, ZS, go, 0)

    def send_states(c):
        r = rates[head_of(c, core, y)]
        a, plane = decay(r, 2.0 * ROWS), decay(r, 2.0 * ROWS * CHIPS)

        def from_planes(i, state):
            at = jnp.where(way == 0, i, ZS - 1 - i)
            wait_bytes(z_recv.at[c, at], zr.at[c, at])
            return plane * state + z_recv[c, at]

        state = lax.fori_loop(0, turn, from_planes, jnp.zeros((SLICE, DH), F32))

        def step(i, state):
            at = jnp.where(way == 0, i, CHIPS - 1 - i)
            s_send[c, at] = state.astype(BF16)
            return a * state + l_recv[c, at].astype(F32)

        lax.fori_loop(0, CHIPS, step, state, unroll=True)
        for dy in (2, 1, 3, 0):
            for dx in (2, 1, 3, 0):
                to_x, to_y = (x + dx) % XS, (y + dy) % YS
                if dx or dy:
                    remote(
                        s_send.at[c, to_x * YS + to_y], s_recv.at[c, y, slice_of(x)], ss.at[c], sr.at[c],
                        in_plane(to_x, to_y),
                    ).start()
        s_recv[c, y, slice_of(x)] = s_send[c, chip]

    def forward(c):
        wait_bytes(l_recv.at[c, pl.ds(0, CHIPS - 1)], sr.at[c])
        remote(s_recv.at[c], x_recv.at[c], xs.at[c], xr.at[c], sibling).start()

    def inside(c, which):
        def one(owner, reads_back):
            head = head_of(c, which, owner)
            r = rates[head]
            cols = cols_of(head)
            row = row_index()
            gap = row - lax.broadcasted_iota(jnp.int32, (ROWS, DH), 1).astype(F32)
            mask = jnp.where(gap >= 0.0, jnp.exp(-r * jnp.maximum(gap, 0.0)), 0.0)
            kh, vh, qh, gh = k[:, cols], v[:, cols], q[:, cols], g[:, cols]
            weights = (dot(gh, vh, (1, 1)) * mask).astype(BF16)
            forwards = (dot(qh, kh, (1, 1)) * mask).astype(BF16)
            grad_q = dot(weights, kh, (1, 0))
            grad_k = dot(weights, qh, (0, 0))
            grad_v = dot(forwards, gh, (0, 0))
            if reads_back:
                before = c_recv[c, 0, owner] if which is core else e_recv[c, owner]
                grad_q += jnp.exp(-r * (row + 1.0)) * dot(gh, before, (1, 1))
            else:
                after = c_recv[c, 1, owner] if which is core else e_recv[c, owner]
                trail = jnp.exp(-r * (ROWS - row))
                grad_k += trail * dot(vh, after, (1, 1))
                grad_v += trail * dot(kh, after, (1, 0))
            dq_in[:, cols] = grad_q
            dk_in[:, cols] = grad_k
            dv_in[:, cols] = grad_v

        for reads_back in (True, False):

            @pl.when(core == int(reads_back))
            def _():
                def body(owner, carry):
                    one(owner, reads_back)
                    return carry

                lax.fori_loop(0, YS, body, 0, unroll=2)

    def inside_own(c):
        inside(c, core)

    def inside_other(c):
        wait_bytes(e_recv.at[c], er.at[c])
        inside(c, 1 - core)

    def finish(c, which, states):
        def one(owner, carry):
            head = head_of(c, which, owner)
            r = rates[head]
            cols = cols_of(head)
            row = row_index() + (core * ROWS).astype(F32)
            lead = jnp.exp(-r * (row + 1.0))
            trail = jnp.exp(-r * (2.0 * ROWS - row))
            before, after = states[c, owner, pl.ds(0, DH)], states[c, owner, pl.ds(DH, DH)]
            dq[:, cols] = (dq_in[:, cols] + lead * dot(g[:, cols], before, (1, 1))).astype(BF16)
            dk[:, cols] = (dk_in[:, cols] + trail * dot(v[:, cols], after, (1, 1))).astype(BF16)
            dv[:, cols] = (dv_in[:, cols] + trail * dot(k[:, cols], after, (1, 0))).astype(BF16)
            return carry

        lax.fori_loop(0, YS, one, 0, unroll=2)

    locals_of(0)
    locals_of(1)
    send_locals(0)
    locals_of(2)
    send_locals(1)
    locals_of(3)
    send_locals(2)
    locals_of(4)
    send_locals(3)
    locals_of(5)
    send_locals(4)
    send_locals(5)
    inside_own(0)
    send_plane(0)
    inside_other(0)
    send_plane(1)
    inside_own(1)
    send_plane(2)
    send_states(0)
    inside_other(1)
    send_plane(3)
    send_states(1)
    inside_own(2)
    send_plane(4)
    send_states(2)
    inside_other(2)
    send_plane(5)
    send_states(3)
    inside_own(3)
    send_states(4)
    inside_other(3)
    inside_own(4)
    send_states(5)
    inside_other(4)
    inside_own(5)
    inside_other(5)
    for c in range(CHUNKS):
        forward(c)
        finish(c, core, s_recv)
        wait_bytes(x_recv.at[c], xr.at[c])
        finish(c, 1 - core, x_recv)

    for c in range(CHUNKS):
        wait_bytes(c_send.at[c], cs.at[c])
        wait_bytes(e_send.at[c], es.at[c])
        wait_bytes(l_recv.at[c, pl.ds(0, CHIPS - 1)], ls.at[c])
        wait_bytes(s_send.at[c, pl.ds(0, CHIPS - 1)], ss.at[c])
        wait_bytes(s_recv.at[c], xs.at[c])

        def sent(i, carry):
            wait_bytes(z_send.at[c], zs.at[c, i])
            return carry

        lax.fori_loop(turn + 1, ZS, sent, 0)


def local(query_rows, key_rows, value_rows, grad_out, decay_rates):
    whole = (ROWS, HEADS * DH)
    sems = pltpu.SemaphoreType.DMA((CHUNKS,))
    anywhere = pl.BlockSpec(memory_space=pl.ANY)
    return pl.pallas_call(
        kernel,
        out_shape=[pltpu.VMEM(whole, BF16)] * 3,
        in_specs=[pl.BlockSpec(memory_space=pltpu.SMEM)] + [anywhere] * 4,
        out_specs=[pl.BlockSpec(memory_space=pltpu.VMEM)] * 3,
        scratch_shapes=[pltpu.VMEM(whole, BF16)] * 4
        + [pltpu.VMEM(whole, F32)] * 3
        + [
            pltpu.VMEM((CHUNKS, YS, 2, DH, DH), F32),
            pltpu.VMEM((CHUNKS, 2, YS, DH, DH), BF16),
            pltpu.VMEM((CHUNKS, 2, YS, DH, DH), BF16),
            pltpu.VMEM((CHUNKS, YS, DH, DH), BF16),
            pltpu.VMEM((CHUNKS, YS, DH, DH), BF16),
            pltpu.VMEM((CHUNKS, YS, 2 * DH, DH), BF16),
            pltpu.VMEM((CHUNKS, CHIPS, SLICE, DH), BF16),
            pltpu.VMEM((CHUNKS, SLICE, DH), F32),
            pltpu.VMEM((CHUNKS, ZS, SLICE, DH), F32),
            pltpu.VMEM((CHUNKS, CHIPS, SLICE, DH), BF16),
            pltpu.VMEM((CHUNKS, YS, 2 * DH, DH), BF16),
            pltpu.VMEM((CHUNKS, YS, 2 * DH, DH), BF16),
            pltpu.SemaphoreType.DMA((CHUNKS, 4)),
        ]
        + [sems] * 6
        + [pltpu.SemaphoreType.DMA((CHUNKS, ZS))] * 2
        + [sems] * 4,
        compiler_params=pltpu.CompilerParams(
            collective_id=0, has_side_effects=True, vmem_limit_bytes=48 * 1024 * 1024
        ),
        name="decayed_attention_backward",
    )(decay_rates, query_rows, key_rows, value_rows, grad_out)


def solution(mesh):
    rows = P(("ctx", "head"), None)
    return jax.shard_map(
        local,
        mesh=mesh,
        in_specs=(rows, rows, rows, rows, P()),
        out_specs=(rows, rows, rows),
        check_vma=False,
    )
```

time: 67.8 us -> 75.4 us (1.11)
  the two profiles are of different devices: /device:TPU:1 before, /device:TPU:6 now
where the time goes in v1:
time: 75.4 us; the launch traced here: 75.3 us
  Pallas kernels  70.5 us (94%)
  local copies, waits for them, and re-layouts  4.08 us (5%)
    pallas_call x1, Pallas kernels, local(): pl.pallas_call(kernel, out_shape=[pltpu.VMEM(whole, BF16)] * 3, in_specs=...  70.5 us
    unnamed x5, local copies, waits for them, and re-layouts  4.08 us

profile of v1, /device:TPU:6, one launch (start us, length us, event | category | flops | bytes accessed | tf_op | source)
XLA Modules:
  0.0 75.3 jit_solution(12609738800502287475)
XLA Ops:
  0.6 0.0 copy-start
  0.6 0.6 copy-done
  1.3 70.5 %decayed_attention_backward.1 = (bf16[128,6144]{1,0:T(8,128)(2,1)S(1)}, bf16[128,6144]{1,0:T(8,128)(2,1)S(1)}, bf16[128,6144]{1,0:T(8,128)(2,1)S(1)}) custom-call(f32[48]{0:T(128)S(1)} %copy-done, bf16[128,6144]{1,0:T(8,128)(2,1)} %q_hbm.1, bf16[128,6144]{1,0:T(8,128)(2,1)} %k_hbm.1, bf16[128,6144]{1,0:T(8,128)(2,1)} %v_hbm.1, bf16[128,6144]{1,0:T(8,128)(2,1)} %g_hbm.1), custom_call_target="tpu_custom_call" | custom-call | tf_op jit(solution)/shard_map/decayed_attention_backward/pallas_call | solution.py:316
  71.8 1.1 %copy.11 = bf16[128,6144]{1,0:T(8,128)(2,1)} copy(bf16[128,6144]{1,0:T(8,128)(2,1)S(1)} %get-tuple-element.3) | data formatting | bytes 3145728
  73.0 1.1 %copy.12 = bf16[128,6144]{1,0:T(8,128)(2,1)} copy(bf16[128,6144]{1,0:T(8,128)(2,1)S(1)} %get-tuple-element.4) | data formatting | bytes 3145728
  74.1 1.1 %copy.13 = bf16[128,6144]{1,0:T(8,128)(2,1)} copy(bf16[128,6144]{1,0:T(8,128)(2,1)S(1)} %get-tuple-element.5) | data formatting | bytes 3145728
Async XLA Ops:
  0.6 0.7 copy-start

commit v2 on v1

v2 whole, which is shorter than its diff:
```python
import jax
import jax.numpy as jnp
from jax import lax
from jax.experimental import pallas as pl
from jax.experimental.pallas import tpu as pltpu
from jax.sharding import PartitionSpec as P

DH = 128
ROWS = 128
HEADS = 48
XS, YS, ZS = 4, 4, 8
CHIPS = XS * YS
SET = YS
CHUNKS = HEADS // (2 * SET)
PART = DH // XS
LAG = 3
PAIRS = 3
LOCAL_UNROLL = 4
PIECES = 1
AHEAD = 5
MESH = pl.DeviceIdType.MESH
F32 = jnp.float32
BF16 = jnp.bfloat16


AWAY = (
    (2, 2), (2, 1), (1, 2), (2, 3), (3, 2), (1, 1), (3, 3), (0, 2), (2, 0), (1, 3), (3, 1), (0, 1), (3, 0), (0, 3), (1, 0),
)


def dot(a, b, dims):
    return lax.dot_general(a, b, ((dims[:1], dims[1:]), ((), ())), preferred_element_type=F32)


def row_index():
    return lax.broadcasted_iota(jnp.int32, (ROWS, DH), 0).astype(F32)


def decay(r, steps):
    return jnp.exp(jnp.full((1, DH), -r * steps, F32))


def remote(src, dst, send, recv, device):
    return pltpu.make_async_remote_copy(
        src_ref=src, dst_ref=dst, send_sem=send, recv_sem=recv, device_id=device, device_id_type=MESH
    )


def wait_bytes(ref, sem):
    pltpu.make_async_copy(ref, ref, sem).wait()


def kernel(
    rates_hbm, q_hbm, k_hbm, v_hbm, g_hbm, dq, dk, dv,
    rates, rate_sem, q, k, v, g, dq_in, dk_in, dv_in,
    own_local, r_send, r_recv, e_send, e_recv, l_send, l_recv, z_send, z_recv, s_send, states,
    load_sem, rs, rr, es, er, ls, lr, zs, zr, ss, sr, xs, xr,
):
    line, place = lax.axis_index("ctx"), lax.axis_index("head")
    z, x = line // XS, line % XS
    y, core = place // 2, place % 2
    chip = x * YS + y
    sibling = (line, place + 1 - 2 * core)

    def in_plane(to):
        return (z * XS + to // YS, (to % YS) * 2 + core)

    def away(dx, dy):
        return (x + jnp.where(core == 0, dx, XS - dx)) % XS, (y + jnp.where(core == 0, dy, YS - dy)) % YS

    def along_z(to_z):
        return (to_z * XS + x, place)

    ins = ((k_hbm, k), (v_hbm, v), (q_hbm, q), (g_hbm, g))

    def load(c, n):
        cols = pl.ds(pl.multiple_of(c * SET * 2 * DH, SET * 2 * DH), SET * 2 * DH)
        return pltpu.make_async_copy(ins[n][0].at[:, cols], ins[n][1].at[:, cols], load_sem.at[c, n])

    def begin(c, carry):
        for n in range(4):
            load(c, n).start()
        return carry

    fetch = pltpu.make_async_copy(rates_hbm, rates, rate_sem)
    fetch.start()
    begin(0, 0)

    barrier = pltpu.get_barrier_semaphore()
    pl.semaphore_signal(barrier, inc=1, device_id=sibling, device_id_type=MESH)

    def greet_plane(d, carry):
        pl.semaphore_signal(barrier, inc=1, device_id=in_plane((chip + d) % CHIPS), device_id_type=MESH)
        return carry

    def greet_z(d, carry):
        pl.semaphore_signal(barrier, inc=1, device_id=along_z((z + d) % ZS), device_id_type=MESH)
        return carry

    lax.fori_loop(1, CHIPS, greet_plane, 0)
    lax.fori_loop(1, ZS, greet_z, 0)
    begin(1, 0)
    fetch.wait()

    def set_of(c, which):
        return (c * 2 + which) * SET

    def cols_of(head):
        return pl.ds(pl.multiple_of(head * DH, DH), DH)

    def local_states(head):
        r = rates[head]
        cols = cols_of(head)
        row = row_index()
        kd = (k[:, cols].astype(F32) * jnp.exp(-r * (ROWS - 1.0 - row))).astype(BF16)
        qd = (q[:, cols].astype(F32) * jnp.exp(-r * row)).astype(BF16)
        return dot(kd, v[:, cols], (0, 0)), dot(qd, g[:, cols], (0, 0))

    def locals_of(c):
        for n in range(4):
            load(c, n).wait()

        @pl.when(c + 2 < CHUNKS)
        def _():
            begin(c + 2, 0)

        def theirs(owner, carry):
            head = set_of(c, 1 - core) + owner
            kv, qd = local_states(head)
            e_send[head] = jnp.where(core == 0, kv, qd).astype(BF16)
            r_send[c, owner] = jnp.where(core == 0, qd, kv).astype(BF16)
            return carry

        lax.fori_loop(0, SET, theirs, 0, unroll=LOCAL_UNROLL)

        @pl.when(c == 0)
        def _():
            pl.semaphore_wait(barrier, 1 + (CHIPS - 1) + (ZS - 1))

        heads = pl.ds(set_of(c, 1 - core), SET)
        remote(e_send.at[heads], e_recv.at[heads], es.at[c, 0], er.at[c, 0], sibling).start()
        remote(r_send.at[c], r_recv.at[c], rs.at[c], rr.at[c], sibling).start()

        def mine(owner, carry):
            head = set_of(c, core) + owner
            kv, qd = local_states(head)
            own_local[c, owner, 0] = kv
            own_local[c, owner, 1] = qd
            e_send[head] = jnp.where(core == 0, kv, qd).astype(BF16)
            return carry

        lax.fori_loop(0, SET, mine, 0, unroll=LOCAL_UNROLL)
        heads = pl.ds(set_of(c, core), SET)
        remote(e_send.at[heads], e_recv.at[heads], es.at[c, 1], er.at[c, 1], sibling).start()

    def send_locals(c):
        wait_bytes(r_recv.at[c], rr.at[c])
        wait_bytes(r_recv.at[c], er.at[c, 0])

        def head_done(i, carry):
            to_y = i
            head = set_of(c, core) + to_y
            half = decay(rates[head], float(ROWS))
            same = own_local[c, to_y, core] * half + r_recv[c, to_y].astype(F32)
            other = own_local[c, to_y, 1 - core] + half * e_recv[head].astype(F32)
            l_send[c, to_y, :, core] = same.astype(BF16).reshape(XS, PART, DH)
            l_send[c, to_y, :, 1 - core] = other.astype(BF16).reshape(XS, PART, DH)

            return carry

        lax.fori_loop(0, YS, head_done, 0)
        for dx, dy in AWAY:
            to_x, to_y = away(dx, dy)
            remote(
                l_send.at[c, to_y, to_x], l_recv.at[c, chip], ls.at[c], lr.at[c], in_plane(to_x * YS + to_y)
            ).start()
        l_recv[c, chip] = l_send[c, y, x]

    def send_plane(c):
        wait_bytes(l_recv.at[c, pl.ds(0, CHIPS - 1)], lr.at[c])
        a = decay(rates[set_of(c, core) + y], 2.0 * ROWS)

        def step(i, both):
            kv, qd = both
            kv = a * kv + l_recv[c, i, 0].astype(F32)
            qd = a * qd + l_recv[c, CHIPS - 1 - i, 1].astype(F32)
            return kv, qd

        zero = jnp.zeros((PART, DH), F32)
        kv, qd = lax.fori_loop(0, CHIPS, step, (zero, zero), unroll=4)
        z_send[c, 0] = kv
        z_send[c, 1] = qd

        def go(d, carry):
            to = (z + d) % ZS
            which = jnp.where(to > z, 0, 1)
            remote(z_send.at[c, which], z_recv.at[c, z], zs.at[c], zr.at[c], along_z(to)).start()
            return carry

        lax.fori_loop(1, ZS, go, 0)

    def send_states(c):
        wait_bytes(z_recv.at[c, pl.ds(0, ZS - 1)], zr.at[c])
        head = set_of(c, core) + y
        a, plane = decay(rates[head], 2.0 * ROWS), decay(rates[head], 2.0 * ROWS * CHIPS)
        zero = jnp.zeros((PART, DH), F32)
        kv = lax.fori_loop(0, z, lambda i, state: plane * state + z_recv[c, i], zero)
        qd = lax.fori_loop(0, ZS - 1 - z, lambda i, state: plane * state + z_recv[c, ZS - 1 - i], zero)

        def step(i, both):
            kv, qd = both
            s_send[c, i, 0] = kv.astype(BF16)
            s_send[c, CHIPS - 1 - i, 1] = qd.astype(BF16)
            kv = a * kv + l_recv[c, i, 0].astype(F32)
            qd = a * qd + l_recv[c, CHIPS - 1 - i, 1].astype(F32)
            return kv, qd

        lax.fori_loop(0, CHIPS, step, (kv, qd), unroll=4)

        for dx, dy in AWAY:
            to_x, to_y = away(dx, dy)
            to = to_x * YS + to_y
            remote(s_send.at[c, to], states.at[head, x], ss.at[c], sr.at[c], in_plane(to)).start()
        states[head, x] = s_send[c, chip]

    def inside(pair, carry):
        def one(head, reads_back):
            r = rates[head]
            cols = cols_of(head)
            row = row_index()
            gap = row - lax.broadcasted_iota(jnp.int32, (ROWS, DH), 1).astype(F32)
            mask = jnp.where(gap >= 0.0, jnp.exp(-r * jnp.maximum(gap, 0.0)), 0.0)
            kh, vh, qh, gh = k[:, cols], v[:, cols], q[:, cols], g[:, cols]
            weights = (dot(gh, vh, (1, 1)) * mask).astype(BF16)
            forwards = (dot(qh, kh, (1, 1)) * mask).astype(BF16)
            grad_q = dot(weights, kh, (1, 0))
            grad_k = dot(weights, qh, (0, 0))
            grad_v = dot(forwards, gh, (0, 0))
            near = e_recv[head]
            if reads_back:
                grad_q += jnp.exp(-r * (row + 1.0)) * dot(gh, near, (1, 1))
            else:
                trail = jnp.exp(-r * (ROWS - row))
                grad_k += trail * dot(vh, near, (1, 1))
                grad_v += trail * dot(kh, near, (1, 0))
            dq_in[:, cols] = grad_q
            dk_in[:, cols] = grad_k
            dv_in[:, cols] = grad_v

        for reads_back in (True, False):

            @pl.when(core == int(reads_back))
            def _():
                one(2 * pair, reads_back)
                one(2 * pair + 1, reads_back)

        return carry

    def finish(first):
        def one(i, carry):
            head = first + i
            r = rates[head]
            cols = cols_of(head)
            row = row_index() + (core * ROWS).astype(F32)
            lead = jnp.exp(-r * (row + 1.0))
            trail = jnp.exp(-r * (2.0 * ROWS - row))
            before = states[head, :, 0].reshape(DH, DH)
            after = states[head, :, 1].reshape(DH, DH)
            dq[:, cols] = (dq_in[:, cols] + lead * dot(g[:, cols], before, (1, 1))).astype(BF16)
            dk[:, cols] = (dk_in[:, cols] + trail * dot(v[:, cols], after, (1, 1))).astype(BF16)
            dv[:, cols] = (dv_in[:, cols] + trail * dot(k[:, cols], after, (1, 0))).astype(BF16)
            return carry

        lax.fori_loop(0, SET, one, 0, unroll=2)

    def first_part(t, carry):
        @pl.when(t < CHUNKS)
        def _():
            locals_of(t)

        @pl.when((t >= 1) & (t <= AHEAD))
        def _():
            send_locals(t - 1)

        return carry

    lax.fori_loop(0, CHUNKS, first_part, 0)

    def arrived(c, carry):
        wait_bytes(r_recv.at[c], er.at[c, 1])
        return carry

    lax.fori_loop(0, CHUNKS, arrived, 0)

    def second_part(t, carry):
        @pl.when(t < CHUNKS)
        def _():
            send_plane(t)

        @pl.when(t + AHEAD < CHUNKS)
        def _():
            send_locals(t + AHEAD)

        @pl.when(t >= LAG)
        def _():
            send_states(t - LAG)

        lax.fori_loop(jnp.minimum(PAIRS * t, HEADS // 2), jnp.minimum(PAIRS * (t + 1), HEADS // 2), inside, 0)
        return carry

    lax.fori_loop(0, CHUNKS + LAG, second_part, 0)

    def third_part(t, carry):
        @pl.when(t >= 1)
        def _():
            wait_bytes(states.at[pl.ds(0, SET)], xr.at[t - 1])
            finish(set_of(t - 1, 1 - core))

        @pl.when(t < CHUNKS)
        def _():
            wait_bytes(l_recv.at[t, pl.ds(0, CHIPS - 1)], sr.at[t])
            heads = pl.ds(set_of(t, core), SET)
            remote(states.at[heads], states.at[heads], xs.at[t], xr.at[t], sibling).start()
            finish(set_of(t, core))

        return carry

    lax.fori_loop(0, CHUNKS + 1, third_part, 0)

    def sent(c, carry):
        wait_bytes(r_send.at[c], rs.at[c])
        wait_bytes(r_send.at[c], es.at[c, 0])
        wait_bytes(r_send.at[c], es.at[c, 1])
        wait_bytes(l_recv.at[c, pl.ds(0, CHIPS - 1)], ls.at[c])
        wait_bytes(s_send.at[c, pl.ds(0, CHIPS - 1)], ss.at[c])
        wait_bytes(states.at[pl.ds(0, SET)], xs.at[c])
        wait_bytes(z_recv.at[c, pl.ds(0, ZS - 1)], zs.at[c])
        return carry

    lax.fori_loop(0, CHUNKS, sent, 0)


def write_out(dq, dk, dv, dq_hbm, dk_hbm, dv_hbm, sems):
    rows = ROWS // PIECES
    copies = [
        pltpu.make_async_copy(here.at[pl.ds(i * rows, rows)], there.at[pl.ds(i * rows, rows)], sems.at[n, i])
        for n, (here, there) in enumerate(((dq, dq_hbm), (dk, dk_hbm), (dv, dv_hbm)))
        for i in range(PIECES)
    ]
    for copy in copies:
        copy.start()
    for copy in copies:
        copy.wait()


def local(query_rows, key_rows, value_rows, grad_out, decay_rates):
    whole = (ROWS, HEADS * DH)
    sems = pltpu.SemaphoreType.DMA((CHUNKS,))
    pair_sems = pltpu.SemaphoreType.DMA((CHUNKS, 2))
    anywhere = pl.BlockSpec(memory_space=pl.ANY)
    grads = pl.pallas_call(
        kernel,
        out_shape=[pltpu.VMEM(whole, BF16)] * 3,
        in_specs=[pl.BlockSpec(memory_space=pltpu.HBM)] + [anywhere] * 4,
        out_specs=[pl.BlockSpec(memory_space=pltpu.VMEM)] * 3,
        scratch_shapes=[pltpu.SMEM((HEADS,), F32), pltpu.SemaphoreType.DMA(())]
        + [pltpu.VMEM(whole, BF16)] * 4
        + [pltpu.VMEM(whole, F32)] * 3
        + [
            pltpu.VMEM((CHUNKS, SET, 2, DH, DH), F32),
            pltpu.VMEM((CHUNKS, SET, DH, DH), BF16),
            pltpu.VMEM((CHUNKS, SET, DH, DH), BF16),
            pltpu.VMEM((HEADS, DH, DH), BF16),
            pltpu.VMEM((HEADS, DH, DH), BF16),
            pltpu.VMEM((CHUNKS, SET, XS, 2, PART, DH), BF16),
            pltpu.VMEM((CHUNKS, CHIPS, 2, PART, DH), BF16),
            pltpu.VMEM((CHUNKS, 2, PART, DH), F32),
            pltpu.VMEM((CHUNKS, ZS, PART, DH), F32),
            pltpu.VMEM((CHUNKS, CHIPS, 2, PART, DH), BF16),
            pltpu.VMEM((HEADS, XS, 2, PART, DH), BF16),
            pltpu.SemaphoreType.DMA((CHUNKS, 4)),
            sems, sems, pair_sems, pair_sems, sems, sems, sems, sems, sems, sems, sems, sems,
        ],
        compiler_params=pltpu.CompilerParams(
            collective_id=0, has_side_effects=True, vmem_limit_bytes=48 * 1024 * 1024
        ),
        name="decayed_attention_backward",
    )(decay_rates, query_rows, key_rows, value_rows, grad_out)
    return pl.pallas_call(
        write_out,
        out_shape=[jax.ShapeDtypeStruct(whole, BF16)] * 3,
        in_specs=[anywhere] * 3,
        out_specs=[anywhere] * 3,
        scratch_shapes=[pltpu.SemaphoreType.DMA((3, PIECES))],
        compiler_params=pltpu.CompilerParams(vmem_limit_bytes=1024 * 1024),
        name="write_gradients",
    )(*grads)


def solution(mesh):
    rows = P(("ctx", "head"), None)
    return jax.shard_map(
        local,
        mesh=mesh,
        in_specs=(rows, rows, rows, rows, P()),
        out_specs=(rows, rows, rows),
        check_vma=False,
    )
```

time: 75.4 us -> 55.8 us (0.74)
  the two profiles are of different devices: /device:TPU:6 before, /device:TPU:1 now
where the time goes in v2:
time: 55.8 us; the launch traced here: 55.6 us
  Pallas kernels  54.4 us (97%)
  local copies, waits for them, and re-layouts  0.65 us (1%)
  between operations  0.65 us (1%)
    pallas_call x1, Pallas kernels, local(): pl.pallas_call(kernel, out_shape=[pltpu.VMEM(whole, BF16)] * 3, in_specs=...  52.1 us
    pallas_call x1, Pallas kernels, local(): pl.pallas_call(write_out, out_shape=[jax.ShapeDtypeStruct(whole, BF16)] *...  2.21 us

profile of v2, /device:TPU:1, one launch (start us, length us, event | category | flops | bytes accessed | tf_op | source)
XLA Modules:
  0.0 55.6 jit_solution(5947440615162063570)
XLA Ops:
  0.6 0.0 copy-start
  0.6 0.6 %copy-done = f32[48]{0:T(128)S(1)} copy-done((f32[48]{0:T(128)S(1)}, f32[48]{0:T(128)}, u32[]{:S(2)}) %copy-start) | copy-done | bytes 216
  1.3 52.1 %decayed_attention_backward.1 = (bf16[128,6144]{1,0:T(8,128)(2,1)S(1)}, bf16[128,6144]{1,0:T(8,128)(2,1)S(1)}, bf16[128,6144]{1,0:T(8,128)(2,1)S(1)}) custom-call(f32[48]{0:T(128)S(1)} %copy-done, bf16[128,6144]{1,0:T(8,128)(2,1)} %q_hbm.1, bf16[128,6144]{1,0:T(8,128)(2,1)} %k_hbm.1, bf16[128,6144]{1,0:T(8,128)(2,1)} %v_hbm.1, bf16[128,6144]{1,0:T(8,128)(2,1)} %g_hbm.1), custom_call_target="tpu_custom_call" | custom-call | tf_op jit(solution)/shard_map/decayed_attention_backward/pallas_call | solution.py:361
  53.4 2.2 %write_gradients.1 = (bf16[128,6144]{1,0:T(8,128)(2,1)}, bf16[128,6144]{1,0:T(8,128)(2,1)}, bf16[128,6144]{1,0:T(8,128)(2,1)}) custom-call(bf16[128,6144]{1,0:T(8,128)(2,1)S(1)} %get-tuple-element.6.dq, bf16[128,6144]{1,0:T(8,128)(2,1)S(1)} %get-tuple-element.7.dk, bf16[128,6144]{1,0:T(8,128)(2,1)S(1)} %get-tuple-element.8.dv), custom_call_target="tpu_custom_call" | custom-call | tf_op jit(solution)/shard_map/write_gradients/pallas_call | solution.py:389
Async XLA Ops:
  0.6 0.7 %copy-start = (f32[48]{0:T(128)S(1)}, f32[48]{0:T(128)}, u32[]{:S(2)}) copy-start(f32[48]{0:T(128)} %rates_hbm.1) | copy-start | bytes 580

commit v3 on v2

--- a/solution.py
+++ b/solution.py
@@ -17,7 +17,7 @@
 PAIRS = 3
 LOCAL_UNROLL = 4
 PIECES = 1
-AHEAD = 5
+AHEAD = 6
 MESH = pl.DeviceIdType.MESH
 F32 = jnp.float32
 BF16 = jnp.bfloat16
@@ -62,11 +62,12 @@
     chip = x * YS + y
     sibling = (line, place + 1 - 2 * core)
 
-    def in_plane(to):
-        return (z * XS + to // YS, (to % YS) * 2 + core)
-
-    def away(dx, dy):
-        return (x + jnp.where(core == 0, dx, XS - dx)) % XS, (y + jnp.where(core == 0, dy, YS - dy)) % YS
+    def in_plane(to_x, to_y):
+        return (z * XS + to_x, to_y * 2 + core)
+
+    xs_away = [lax.rem(x + jnp.where(core == 0, d, (XS - d) % XS), XS) for d in range(XS)]
+    ys_away = [lax.rem(y + jnp.where(core == 0, d, (YS - d) % YS), YS) for d in range(YS)]
+    zs_away = [lax.rem(z + jnp.where(core == 0, d, (ZS - d) % ZS), ZS) for d in range(ZS)]
 
     def along_z(to_z):
         return (to_z * XS + x, place)
@@ -89,16 +90,11 @@
     barrier = pltpu.get_barrier_semaphore()
     pl.semaphore_signal(barrier, inc=1, device_id=sibling, device_id_type=MESH)
 
-    def greet_plane(d, carry):
-        pl.semaphore_signal(barrier, inc=1, device_id=in_plane((chip + d) % CHIPS), device_id_type=MESH)
-        return carry
-
-    def greet_z(d, carry):
-        pl.semaphore_signal(barrier, inc=1, device_id=along_z((z + d) % ZS), device_id_type=MESH)
-        return carry
-
-    lax.fori_loop(1, CHIPS, greet_plane, 0)
-    lax.fori_loop(1, ZS, greet_z, 0)
+    for dx, dy in AWAY:
+        to = in_plane(xs_away[dx], ys_away[dy])
+        pl.semaphore_signal(barrier, inc=1, device_id=to, device_id_type=MESH)
+    for d in range(1, ZS):
+        pl.semaphore_signal(barrier, inc=1, device_id=along_z(zs_away[d]), device_id_type=MESH)
     begin(1, 0)
     fetch.wait()
 
@@ -168,11 +164,11 @@
 
             return carry
 
-        lax.fori_loop(0, YS, head_done, 0)
+        lax.fori_loop(0, YS, head_done, 0, unroll=2)
         for dx, dy in AWAY:
-            to_x, to_y = away(dx, dy)
+            to_x, to_y = xs_away[dx], ys_away[dy]
             remote(
-                l_send.at[c, to_y, to_x], l_recv.at[c, chip], ls.at[c], lr.at[c], in_plane(to_x * YS + to_y)
+                l_send.at[c, to_y, to_x], l_recv.at[c, chip], ls.at[c], lr.at[c], in_plane(to_x, to_y)
             ).start()
         l_recv[c, chip] = l_send[c, y, x]
 
@@ -187,17 +183,14 @@
             return kv, qd
 
         zero = jnp.zeros((PART, DH), F32)
-        kv, qd = lax.fori_loop(0, CHIPS, step, (zero, zero), unroll=4)
+        kv, qd = lax.fori_loop(0, CHIPS, step, (zero, zero), unroll=True)
         z_send[c, 0] = kv
         z_send[c, 1] = qd
 
-        def go(d, carry):
-            to = (z + d) % ZS
+        for d in (4, 3, 5, 2, 6, 1, 7):
+            to = zs_away[d]
             which = jnp.where(to > z, 0, 1)
             remote(z_send.at[c, which], z_recv.at[c, z], zs.at[c], zr.at[c], along_z(to)).start()
-            return carry
-
-        lax.fori_loop(1, ZS, go, 0)
 
     def send_states(c):
         wait_bytes(z_recv.at[c, pl.ds(0, ZS - 1)], zr.at[c])
@@ -215,12 +208,12 @@
             qd = a * qd + l_recv[c, CHIPS - 1 - i, 1].astype(F32)
             return kv, qd
 
-        lax.fori_loop(0, CHIPS, step, (kv, qd), unroll=4)
+        lax.fori_loop(0, CHIPS, step, (kv, qd), unroll=True)
 
         for dx, dy in AWAY:
-            to_x, to_y = away(dx, dy)
-            to = to_x * YS + to_y
-            remote(s_send.at[c, to], states.at[head, x], ss.at[c], sr.at[c], in_plane(to)).start()
+            to_x, to_y = xs_away[dx], ys_away[dy]
+            landing = states.at[head, x]
+            remote(s_send.at[c, to_x * YS + to_y], landing, ss.at[c], sr.at[c], in_plane(to_x, to_y)).start()
         states[head, x] = s_send[c, chip]
 
     def inside(pair, carry):
@@ -271,7 +264,7 @@
             dv[:, cols] = (dv_in[:, cols] + trail * dot(k[:, cols], after, (1, 0))).astype(BF16)
             return carry
 
-        lax.fori_loop(0, SET, one, 0, unroll=2)
+        lax.fori_loop(0, SET, one, 0, unroll=4)
 
     def first_part(t, carry):
         @pl.when(t < CHUNKS)
@@ -284,7 +277,7 @@
 
         return carry
 
-    lax.fori_loop(0, CHUNKS, first_part, 0)
+    lax.fori_loop(0, CHUNKS + 1, first_part, 0)
 
     def arrived(c, carry):
         wait_bytes(r_recv.at[c], er.at[c, 1])
@@ -296,10 +289,6 @@
         @pl.when(t < CHUNKS)
         def _():
             send_plane(t)
-
-        @pl.when(t + AHEAD < CHUNKS)
-        def _():
-            send_locals(t + AHEAD)
 
         @pl.when(t >= LAG)
         def _():
@@ -382,7 +371,7 @@
             sems, sems, pair_sems, pair_sems, sems, sems, sems, sems, sems, sems, sems, sems,
         ],
         compiler_params=pltpu.CompilerParams(
-            collective_id=0, has_side_effects=True, vmem_limit_bytes=48 * 1024 * 1024
+            collective_id=0, has_side_effects=True, vmem_limit_bytes=57392 * 1024
         ),
         name="decayed_attention_backward",
     )(decay_rates, query_rows, key_rows, value_rows, grad_out)

time: 55.8 us -> 55.1 us (0.987)
  local copies, waits for them, and re-layouts: 0.65 us -> 0 us
    unnamed x2 -> x0, local copies, waits for them, and re-layouts: 0.65 us -> none
where the time goes in v3:
time: 55.1 us; the launch traced here: 55 us
  Pallas kernels  54.3 us (99%)
  between operations  0.64 us (1%)
    pallas_call x1, Pallas kernels, local(): pl.pallas_call(kernel, out_shape=[pltpu.VMEM(whole, BF16)] * 3, in_specs=...  52.1 us
    pallas_call x1, Pallas kernels, local(): pl.pallas_call(write_out, out_shape=[jax.ShapeDtypeStruct(whole, BF16)] *...  2.21 us

profile of v3, /device:TPU:1, one launch (start us, length us, event | category | flops | bytes accessed | tf_op | source)
XLA Modules:
  0.0 55.0 jit_solution(866914681372450395)
XLA Ops:
  0.6 52.1 %decayed_attention_backward.1 = (bf16[128,6144]{1,0:T(8,128)(2,1)S(1)}, bf16[128,6144]{1,0:T(8,128)(2,1)S(1)}, bf16[128,6144]{1,0:T(8,128)(2,1)S(1)}) custom-call(f32[48]{0:T(128)} %rates_hbm.1, bf16[128,6144]{1,0:T(8,128)(2,1)} %q_hbm.1, bf16[128,6144]{1,0:T(8,128)(2,1)} %k_hbm.1, bf16[128,6144]{1,0:T(8,128)(2,1)} %v_hbm.1, bf16[128,6144]{1,0:T(8,128)(2,1)} %g_hbm.1), custom_call_target="tpu_custom_call" | custom-call | tf_op jit(solution)/shard_map/decayed_attention_backward/pallas_call | solution.py:350
  52.7 2.2 %write_gradients.1 = (bf16[128,6144]{1,0:T(8,128)(2,1)}, bf16[128,6144]{1,0:T(8,128)(2,1)}, bf16[128,6144]{1,0:T(8,128)(2,1)}) custom-call(bf16[128,6144]{1,0:T(8,128)(2,1)S(1)} %get-tuple-element.6.dq, bf16[128,6144]{1,0:T(8,128)(2,1)S(1)} %get-tuple-element.7.dk, bf16[128,6144]{1,0:T(8,128)(2,1)S(1)} %get-tuple-element.8.dv), custom_call_target="tpu_custom_call" | custom-call | tf_op jit(solution)/shard_map/write_gradients/pallas_call | solution.py:378

commit v4 on v3

--- a/solution.py
+++ b/solution.py
@@ -153,8 +153,7 @@
         wait_bytes(r_recv.at[c], rr.at[c])
         wait_bytes(r_recv.at[c], er.at[c, 0])
 
-        def head_done(i, carry):
-            to_y = i
+        def head_done(to_y):
             head = set_of(c, core) + to_y
             half = decay(rates[head], float(ROWS))
             same = own_local[c, to_y, core] * half + r_recv[c, to_y].astype(F32)
@@ -162,14 +161,15 @@
             l_send[c, to_y, :, core] = same.astype(BF16).reshape(XS, PART, DH)
             l_send[c, to_y, :, 1 - core] = other.astype(BF16).reshape(XS, PART, DH)
 
-            return carry
-
-        lax.fori_loop(0, YS, head_done, 0, unroll=2)
-        for dx, dy in AWAY:
-            to_x, to_y = xs_away[dx], ys_away[dy]
-            remote(
-                l_send.at[c, to_y, to_x], l_recv.at[c, chip], ls.at[c], lr.at[c], in_plane(to_x, to_y)
-            ).start()
+
+        for dy, steps in ((2, (2, 1, 3, 0)), (1, (2, 3, 1, 0)), (3, (2, 1, 3, 0)), (0, (2, 1, 3))):
+            to_y = ys_away[dy]
+            head_done(to_y)
+            for dx in steps:
+                to_x = xs_away[dx]
+                remote(
+                    l_send.at[c, to_y, to_x], l_recv.at[c, chip], ls.at[c], lr.at[c], in_plane(to_x, to_y)
+                ).start()
         l_recv[c, chip] = l_send[c, y, x]
 
     def send_plane(c):

time: 55.1 us -> 55 us (level)
  no operation moved by 1% of the time
where the time goes in v4:
time: 55 us; the launch traced here: 54.9 us
  Pallas kernels  54.2 us (99%)
  between operations  0.64 us (1%)
    pallas_call x1, Pallas kernels, local(): pl.pallas_call(kernel, out_shape=[pltpu.VMEM(whole, BF16)] * 3, in_specs=...  52 us
    pallas_call x1, Pallas kernels, local(): pl.pallas_call(write_out, out_shape=[jax.ShapeDtypeStruct(whole, BF16)] *...  2.21 us

profile of v4, /device:TPU:1, one launch (start us, length us, event | category | flops | bytes accessed | tf_op | source)
XLA Modules:
  0.0 54.9 jit_solution(15778263675693926118)
XLA Ops:
  0.6 52.0 %decayed_attention_backward.1 = (bf16[128,6144]{1,0:T(8,128)(2,1)S(1)}, bf16[128,6144]{1,0:T(8,128)(2,1)S(1)}, bf16[128,6144]{1,0:T(8,128)(2,1)S(1)}) custom-call(f32[48]{0:T(128)} %rates_hbm.1, bf16[128,6144]{1,0:T(8,128)(2,1)} %q_hbm.1, bf16[128,6144]{1,0:T(8,128)(2,1)} %k_hbm.1, bf16[128,6144]{1,0:T(8,128)(2,1)} %v_hbm.1, bf16[128,6144]{1,0:T(8,128)(2,1)} %g_hbm.1), custom_call_target="tpu_custom_call" | custom-call | tf_op jit(solution)/shard_map/decayed_attention_backward/pallas_call | solution.py:350
  52.7 2.2 %write_gradients.1 = (bf16[128,6144]{1,0:T(8,128)(2,1)}, bf16[128,6144]{1,0:T(8,128)(2,1)}, bf16[128,6144]{1,0:T(8,128)(2,1)}) custom-call(bf16[128,6144]{1,0:T(8,128)(2,1)S(1)} %get-tuple-element.6.dq, bf16[128,6144]{1,0:T(8,128)(2,1)S(1)} %get-tuple-element.7.dk, bf16[128,6144]{1,0:T(8,128)(2,1)S(1)} %get-tuple-element.8.dv), custom_call_target="tpu_custom_call" | custom-call | tf_op jit(solution)/shard_map/write_gradients/pallas_call | solution.py:378

commit v5 on v3

--- a/solution.py
+++ b/solution.py
@@ -213,7 +213,7 @@
         for dx, dy in AWAY:
             to_x, to_y = xs_away[dx], ys_away[dy]
             landing = states.at[head, x]
-            remote(s_send.at[c, to_x * YS + to_y], landing, ss.at[c], sr.at[c], in_plane(to_x, to_y)).start()
+            remote(s_send.at[c, to_x * YS + to_y], landing, ss.at[c], sr.at[c, y], in_plane(to_x, to_y)).start()
         states[head, x] = s_send[c, chip]
 
     def inside(pair, carry):
@@ -249,9 +249,8 @@
 
         return carry
 
-    def finish(first):
-        def one(i, carry):
-            head = first + i
+    def finish(heads):
+        for head in heads:
             r = rates[head]
             cols = cols_of(head)
             row = row_index() + (core * ROWS).astype(F32)
@@ -262,9 +261,6 @@
             dq[:, cols] = (dq_in[:, cols] + lead * dot(g[:, cols], before, (1, 1))).astype(BF16)
             dk[:, cols] = (dk_in[:, cols] + trail * dot(v[:, cols], after, (1, 1))).astype(BF16)
             dv[:, cols] = (dv_in[:, cols] + trail * dot(k[:, cols], after, (1, 0))).astype(BF16)
-            return carry
-
-        lax.fori_loop(0, SET, one, 0, unroll=4)
 
     def first_part(t, carry):
         @pl.when(t < CHUNKS)
@@ -302,15 +298,25 @@
     def third_part(t, carry):
         @pl.when(t >= 1)
         def _():
-            wait_bytes(states.at[pl.ds(0, SET)], xr.at[t - 1])
-            finish(set_of(t - 1, 1 - core))
+            for steps in ((2, 1), (3, 0)):
+                heads = []
+                for dy in steps:
+                    heads.append(set_of(t - 1, 1 - core) + ys_away[dy])
+                    wait_bytes(states.at[heads[-1]], xr.at[t - 1, ys_away[dy]])
+                finish(heads)
 
         @pl.when(t < CHUNKS)
         def _():
-            wait_bytes(l_recv.at[t, pl.ds(0, CHIPS - 1)], sr.at[t])
-            heads = pl.ds(set_of(t, core), SET)
-            remote(states.at[heads], states.at[heads], xs.at[t], xr.at[t], sibling).start()
-            finish(set_of(t, core))
+            for steps in ((2, 1), (3, 0)):
+                heads = []
+                for dy in steps:
+                    owner = ys_away[(YS - dy) % YS]
+                    head = set_of(t, core) + owner
+                    heads.append(head)
+                    came = states.at[head] if dy else states.at[head, pl.ds(0, XS - 1)]
+                    wait_bytes(came, sr.at[t, owner])
+                    remote(states.at[head], states.at[head], xs.at[t, owner], xr.at[t, owner], sibling).start()
+                finish(heads)
 
         return carry
 
@@ -322,7 +328,8 @@
         wait_bytes(r_send.at[c], es.at[c, 1])
         wait_bytes(l_recv.at[c, pl.ds(0, CHIPS - 1)], ls.at[c])
         wait_bytes(s_send.at[c, pl.ds(0, CHIPS - 1)], ss.at[c])
-        wait_bytes(states.at[pl.ds(0, SET)], xs.at[c])
+        for owner in range(YS):
+            wait_bytes(states.at[owner], xs.at[c, owner])
         wait_bytes(z_recv.at[c, pl.ds(0, ZS - 1)], zs.at[c])
         return carry
 
@@ -345,6 +352,7 @@
 def local(query_rows, key_rows, value_rows, grad_out, decay_rates):
     whole = (ROWS, HEADS * DH)
     sems = pltpu.SemaphoreType.DMA((CHUNKS,))
+    owner_sems = pltpu.SemaphoreType.DMA((CHUNKS, SET))
     pair_sems = pltpu.SemaphoreType.DMA((CHUNKS, 2))
     anywhere = pl.BlockSpec(memory_space=pl.ANY)
     grads = pl.pallas_call(
@@ -368,7 +376,7 @@
             pltpu.VMEM((CHUNKS, CHIPS, 2, PART, DH), BF16),
             pltpu.VMEM((HEADS, XS, 2, PART, DH), BF16),
             pltpu.SemaphoreType.DMA((CHUNKS, 4)),
-            sems, sems, pair_sems, pair_sems, sems, sems, sems, sems, sems, sems, sems, sems,
+            sems, sems, pair_sems, pair_sems, sems, sems, sems, sems, sems, owner_sems, owner_sems, owner_sems,
         ],
         compiler_params=pltpu.CompilerParams(
             collective_id=0, has_side_effects=True, vmem_limit_bytes=57392 * 1024

time: 55.1 us -> 55.5 us (level)
  no operation moved by 1% of the time
where the time goes in v5:
time: 55.5 us; the launch traced here: 55.4 us
  Pallas kernels  54.8 us (99%)
  between operations  0.64 us (1%)
    pallas_call x1, Pallas kernels, local(): pl.pallas_call(kernel, out_shape=[pltpu.VMEM(whole, BF16)] * 3, in_specs=...  52.5 us
    pallas_call x1, Pallas kernels, local(): pl.pallas_call(write_out, out_shape=[jax.ShapeDtypeStruct(whole, BF16)] *...  2.21 us

profile of v5, /device:TPU:1, one launch (start us, length us, event | category | flops | bytes accessed | tf_op | source)
XLA Modules:
  0.0 55.4 jit_solution(8690034656264903258)
XLA Ops:
  0.6 52.5 %decayed_attention_backward.1 = (bf16[128,6144]{1,0:T(8,128)(2,1)S(1)}, bf16[128,6144]{1,0:T(8,128)(2,1)S(1)}, bf16[128,6144]{1,0:T(8,128)(2,1)S(1)}) custom-call(f32[48]{0:T(128)} %rates_hbm.1, bf16[128,6144]{1,0:T(8,128)(2,1)} %q_hbm.1, bf16[128,6144]{1,0:T(8,128)(2,1)} %k_hbm.1, bf16[128,6144]{1,0:T(8,128)(2,1)} %v_hbm.1, bf16[128,6144]{1,0:T(8,128)(2,1)} %g_hbm.1), custom_call_target="tpu_custom_call" | custom-call | tf_op jit(solution)/shard_map/decayed_attention_backward/pallas_call | solution.py:358
  53.2 2.2 %write_gradients.1 = (bf16[128,6144]{1,0:T(8,128)(2,1)}, bf16[128,6144]{1,0:T(8,128)(2,1)}, bf16[128,6144]{1,0:T(8,128)(2,1)}) custom-call(bf16[128,6144]{1,0:T(8,128)(2,1)S(1)} %get-tuple-element.6.dq, bf16[128,6144]{1,0:T(8,128)(2,1)S(1)} %get-tuple-element.7.dk, bf16[128,6144]{1,0:T(8,128)(2,1)S(1)} %get-tuple-element.8.dv), custom_call_target="tpu_custom_call" | custom-call | tf_op jit(solution)/shard_map/write_gradients/pallas_call | solution.py:386
